TPU v7x, 256 devices: a whole 4x4x8 slice. The times are simulated.
256 devices in a mesh: dp: 2 (over z_hi), seq: 64 (over z_lo, x, y), head: 2 (over core).
Axes of the slice: x: 4, y: 4, z: 8 (z_hi: 2, z_lo: 4; z = z_hi * 4 + z_lo), core: 2. Of those that a mesh axis runs over, the one named last changes fastest.
Arguments:
- fine_queries: bfloat16 [2, 24576, 32, 128], P('dp', 'seq', 'head'), may hold values from -96 to 96
- fine_keys: bfloat16 [2, 24576, 32, 128], P('dp', 'seq', 'head'), may hold values from -10 to 10
- fine_values: bfloat16 [2, 24576, 32, 128], P('dp', 'seq', 'head'), may hold values from -6 to 6
- coarse_keys: bfloat16 [2, 256, 32, 128], P('dp', 'seq', 'head'), may hold values from -8 to 8
- coarse_values: bfloat16 [2, 256, 32, 128], P('dp', 'seq', 'head'), may hold values from -6 to 6
- out_grad: bfloat16 [2, 24576, 32, 128], P('dp', 'seq', 'head'), may hold values from -6 to 6
Outputs:
- attended: bfloat16 [2, 24576, 32, 128], P('dp', 'seq', 'head')
- query_grad: bfloat16 [2, 24576, 32, 128], P('dp', 'seq', 'head')
- key_grad: bfloat16 [2, 24576, 32, 128], P('dp', 'seq', 'head')
- value_grad: bfloat16 [2, 24576, 32, 128], P('dp', 'seq', 'head')
All inputs are finite; a program needn't handle non-finite values.
Results may differ from a plain program's by a relative error of at most 0.012.
Values may be sent and summed in bfloat16 or wider, within the bound.
No kernel may reach another device: no remote copies, remote signals or barrier semaphores. Data moves between devices by JAX's collectives and lax.ppermute only.
A program may use at most 128 MiB of HBM per device.

v0:
```python
import functools

import jax
import jax.numpy as jnp
from jax import lax
from jax.experimental import pallas as pl
from jax.experimental.pallas import tpu as pltpu
from jax.sharding import PartitionSpec as P

TILE_H = 24
TILE_W = 16
RADIUS = 4
TILES_X = 8
TOKENS = TILE_H * TILE_W
EDGE = RADIUS * TILE_W
SIDE = TILE_H * RADIUS
CORNER = RADIUS * RADIUS
STRIP = SIDE + 2 * CORNER
CHUNKS = 2
BLOCK_ROWS = 8
BLOCKS = TILE_H // BLOCK_ROWS
QUERIES = BLOCK_ROWS * TILE_W
WIN_ROWS = BLOCK_ROWS + 2 * RADIUS
NEAR = WIN_ROWS * (TILE_W + 2 * RADIUS)
FLOOR = -1e30
LOG2E = 1.4426950408889634
BF = jnp.bfloat16
F32 = jnp.float32
SMEM = pl.BlockSpec(memory_space=pltpu.SMEM)
VMEM = pl.BlockSpec(memory_space=pltpu.VMEM)
PARAMS = pltpu.CompilerParams(vmem_limit_bytes=63 << 20)


def nt(a, b):
    return lax.dot_general(a, b, (((1,), (1,)), ((), ())), preferred_element_type=F32)


def tn(a, b):
    return lax.dot_general(a, b, (((0,), (0,)), ((), ())), preferred_element_type=F32)


def nn(a, b):
    return lax.dot_general(a, b, (((1,), (0,)), ((), ())), preferred_element_type=F32)


def sds(*shape):
    return jax.ShapeDtypeStruct(shape, BF)


def exchange(value, rows, which):
    count = lax.axis_size("seq")
    pairs = []
    for source in range(count):
        row, col = divmod(source, TILES_X)
        place, extent = (row, count // TILES_X) if rows else (col, TILES_X)
        target = ((place + which) ^ 1) - which
        if not 0 <= target < extent:
            pairs.append((source, source ^ 1 if rows else source ^ (2 * TILES_X)))
        else:
            pairs.append((source, target * TILES_X + col if rows else row * TILES_X + target))
    return lax.ppermute(value, "seq", pairs)


def widened(block, stride):
    count = lax.axis_size("seq")

    def swapped(mask):
        pairs = [(source, source ^ (mask * stride)) for source in range(count)]
        return lax.ppermute(block, "seq", pairs)

    return [block] + [swapped(mask) for mask in (1, 2, 3)]


def pairs_to_heads_kernel(k, v, kv):
    for i, x in enumerate((k, v)):
        kv[:, i] = jnp.swapaxes(x[0], 0, 1)


def pairs_to_heads(k, v):
    t, h, d = k.shape[1:]
    return pl.pallas_call(
        pairs_to_heads_kernel,
        out_shape=sds(h, 2, t, d),
        compiler_params=PARAMS,
        name="pairs_to_heads",
    )(k, v)


def to_heads_kernel(x, y, a, b):
    a[...] = jnp.swapaxes(x[0], 0, 1)
    b[...] = jnp.swapaxes(y[0], 0, 1)


def to_heads(x, y):
    t, h, d = x.shape[1:]
    return pl.pallas_call(
        to_heads_kernel,
        out_shape=[sds(h, t, d)] * 2,
        compiler_params=PARAMS,
        name="to_heads",
    )(x, y)


def halo_to_heads_kernel(even, x, y, up, dn):
    a = jnp.swapaxes(x[:, 0], 0, 1)
    b = jnp.swapaxes(y[:, 0], 0, 1)
    up[:, 0] = lax.select(even[0] == 1, b, a)
    dn[:, 0] = lax.select(even[0] == 1, a, b)


def halo_to_heads(even, x, y):
    t, _, h, d = x.shape
    tokens = pl.BlockSpec((t, 1, h, d), lambda g: (0, g, 0, 0))
    heads = pl.BlockSpec((h, 1, t, d), lambda g: (0, g, 0, 0))
    return pl.pallas_call(
        halo_to_heads_kernel,
        grid=(2,),
        in_specs=[SMEM, tokens, tokens],
        out_specs=[heads, heads],
        out_shape=[sds(h, 2, t, d)] * 2,
        compiler_params=PARAMS,
        name="halo_to_heads",
    )(even, x, y)


def far_kernel(*refs):
    out = refs[-1]
    n = refs[0].shape[0]
    for j, piece in enumerate(refs[:-1]):
        out[:, 0, j * n : (j + 1) * n] = jnp.swapaxes(piece[:, 0], 0, 1)


def far_heads(pieces):
    n, _, h, d = pieces[0].shape
    t = n * len(pieces)
    return pl.pallas_call(
        far_kernel,
        grid=(2,),
        in_specs=[pl.BlockSpec((n, 1, h, d), lambda g: (0, g, 0, 0))] * len(pieces),
        out_specs=pl.BlockSpec((h, 1, t, d), lambda g: (0, g, 0, 0)),
        out_shape=sds(h, 2, t, d),
        compiler_params=PARAMS,
        name="far_heads",
    )(*pieces)


def sides_kernel(even, a, b, ka, kb, va, vb, *outs):
    h, d = a.shape[2:]
    n = h // CHUNKS
    for j, (mine, e) in enumerate((((ka, va), even[1]), ((kb, vb), 1 - even[1]))):
        for i in range(2):
            x = mine[i][...].reshape(SIDE, h, d)
            for c in range(CHUNKS):
                outs[j * CHUNKS + c][CORNER : CORNER + SIDE, i] = x[:, c * n : (c + 1) * n]
            for g, rows in enumerate((a, b)):
                end = (STRIP - CORNER) * (g ^ even[0])
                for r in range(RADIUS):
                    x = rows[pl.ds(r * TILE_W + (TILE_W - RADIUS) * e, RADIUS), i]
                    for c in range(CHUNKS):
                        outs[j * CHUNKS + c][pl.ds(end + r * RADIUS, RADIUS), i] = x[:, c * n : (c + 1) * n]


def sides(even, a, b, k, v):
    h, d = a.shape[2:]
    k = k.reshape(TILE_H, TILE_W, h, d)
    v = v.reshape(TILE_H, TILE_W, h, d)
    block = (TILE_H, RADIUS, h, d)
    last = TILE_W // RADIUS - 1
    whole = pl.BlockSpec(a.shape, lambda g, e: (0, 0, 0, 0))
    side_a = pl.BlockSpec(block, lambda g, e: (0, last * e[1], 0, 0))
    side_b = pl.BlockSpec(block, lambda g, e: (0, last * (1 - e[1]), 0, 0))
    shape = (STRIP, 2, h // CHUNKS, d)
    outs = pl.pallas_call(
        sides_kernel,
        grid_spec=pltpu.PrefetchScalarGridSpec(
            num_scalar_prefetch=1,
            grid=(1,),
            in_specs=[whole, whole, side_a, side_b, side_a, side_b],
            out_specs=[pl.BlockSpec(shape, lambda g, e: (0, 0, 0, 0))] * (2 * CHUNKS),
        ),
        out_shape=[sds(*shape)] * (2 * CHUNKS),
        compiler_params=PARAMS,
        name="sides",
    )(even, a, b, k, k, v, v)
    return outs[:CHUNKS], outs[CHUNKS:]


def to_tokens_kernel(*refs):
    n = (len(refs) - 2) // 2
    for j in range(2):
        x = jnp.concatenate([r[...] for r in refs[j * n : (j + 1) * n]], 0)
        refs[2 * n + j][0] = jnp.swapaxes(x, 0, 1)


def to_tokens(xs, ys):
    h, t, d = xs[0].shape
    return pl.pallas_call(
        to_tokens_kernel,
        out_shape=[sds(1, t, h * len(xs), d)] * 2,
        compiler_params=PARAMS,
        name="to_tokens",
    )(*xs, *ys)


def fold_kernel(even, *refs):
    gup, gdn, from_a, from_b = (refs[c * CHUNKS : (c + 1) * CHUNKS] for c in range(4))
    a, b = refs[4 * CHUNKS :]
    t, _, h, d = a.shape

    def tokens(parts, rows, cols):
        x = jnp.concatenate([r[:, 0, rows] for r in parts], 0)
        return jnp.swapaxes(x, 0, 1).astype(F32).reshape(RADIUS, cols, h, d)

    folded = []
    for g, o in ((gup, 0), (gdn, STRIP - CORNER)):
        x = tokens(g, slice(0, t), TILE_W)
        sa, sb = (tokens(s, slice(o, o + CORNER), RADIUS) for s in (from_a, from_b))
        left = lax.select(even[1] == 1, sb, sa)
        right = lax.select(even[1] == 1, sa, sb)
        x = jnp.concatenate(
            [x[:, :RADIUS] + left, x[:, RADIUS : TILE_W - RADIUS], x[:, TILE_W - RADIUS :] + right], 1
        )
        folded.append(x.reshape(t, h, d).astype(BF))
    a[:, 0] = lax.select(even[0] == 1, folded[1], folded[0])
    b[:, 0] = lax.select(even[0] == 1, folded[0], folded[1])


def fold(even, gup, gdn, from_a, from_b):
    args = (*gup, *gdn, *from_a, *from_b)
    h, _, t, d = gup[0].shape
    h *= CHUNKS
    return pl.pallas_call(
        fold_kernel,
        grid=(2,),
        in_specs=[SMEM]
        + [pl.BlockSpec((x.shape[0], 1) + x.shape[2:], lambda g: (0, g, 0, 0)) for x in args],
        out_specs=[pl.BlockSpec((t, 1, h, d), lambda g: (0, g, 0, 0))] * 2,
        out_shape=[sds(t, 2, h, d)] * 2,
        compiler_params=PARAMS,
        name="fold",
    )(even, *args)


def premerge_kernel(even, *refs):
    own, from_a, from_b = (refs[c * CHUNKS : (c + 1) * CHUNKS] for c in range(3))
    for i, out in enumerate(refs[3 * CHUNKS :]):
        h, d = out.shape[2:]

        def tokens(parts, rows, *lead):
            x = jnp.concatenate([r[:, i, rows] for r in parts], 0)
            return jnp.swapaxes(x, 0, 1).astype(F32).reshape(*lead, h, d)

        t = tokens(own, slice(0, TOKENS), TILE_H, TILE_W)
        sa = tokens(from_a, slice(CORNER, CORNER + SIDE), TILE_H, RADIUS)
        sb = tokens(from_b, slice(CORNER, CORNER + SIDE), TILE_H, RADIUS)
        le = lax.select(even[1] == 1, sb, sa)
        ri = lax.select(even[1] == 1, sa, sb)
        t = jnp.concatenate(
            [t[:, :RADIUS] + le, t[:, RADIUS : TILE_W - RADIUS], t[:, TILE_W - RADIUS :] + ri], 1
        )
        out[0] = t.reshape(TOKENS, h, d).astype(BF)


def premerge(even, own, from_a, from_b):
    h, _, t, d = own[0].shape
    return pl.pallas_call(
        premerge_kernel,
        in_specs=[SMEM] + [VMEM] * (3 * CHUNKS),
        out_shape=[sds(1, t, h * CHUNKS, d)] * 2,
        compiler_params=PARAMS,
        name="premerge",
    )(even, *own, *from_a, *from_b)


def finish_kernel(even, dk, dv, from_a, from_b, dk_out, dv_out):
    for g, part in enumerate((from_a, from_b)):

        @pl.when(pl.program_id(0) == g)
        def _():
            for i, (x, out) in enumerate(((dk, dk_out), (dv, dv_out))):
                out[0] = (x[0].astype(F32) + part[:, i].astype(F32)).astype(BF)


def finish(even, dk, dv, from_a, from_b):
    h, d = dk.shape[2:]
    last = TOKENS // EDGE - 1
    rows = pl.BlockSpec((1, EDGE, h, d), lambda g, e: (0, last * (g ^ e[0]), 0, 0))
    part = pl.BlockSpec(from_a.shape, lambda g, e: (0, 0, 0, 0))
    return pl.pallas_call(
        finish_kernel,
        grid_spec=pltpu.PrefetchScalarGridSpec(
            num_scalar_prefetch=1,
            grid=(2,),
            in_specs=[rows, rows, part, part],
            out_specs=[rows, rows],
        ),
        out_shape=[sds(*dk.shape)] * 2,
        input_output_aliases={1: 0, 2: 1},
        compiler_params=PARAMS,
        name="finish",
    )(even, dk, dv, from_a, from_b)


def attend_kernel(
    heads, q, do, kv, up, dn, far, sa, sb, bias, even, att, dq, own, gup, gdn, ga, gb, strips_lr
):
    @pl.when(pl.program_id(0) == 0)
    def _():
        for src, side in ((sa, even[1]), (sb, 1 - even[1])):
            for i in range(2):
                strips_lr[side, :, i] = jnp.swapaxes(src[:, i], 0, 1)

    first = pl.program_id(0) * heads
    scale = q.shape[-1] ** -0.5
    half = WIN_ROWS * RADIUS
    mid = WIN_ROWS * TILE_W

    def strips(h, i):
        center = jnp.concatenate([up[h, i], kv[h, i], dn[h, i]], 0)
        return center, strips_lr[0, first + h, i], strips_lr[1, first + h, i], far[h, i]

    def window(parts, b):
        c, l, r, f = parts
        o, s = b * BLOCK_ROWS * TILE_W, b * BLOCK_ROWS * RADIUS
        return jnp.concatenate([c[o : o + mid], l[s : s + half], r[s : s + half], f], 0)

    parts = [[strips(h, i) for i in range(2)] for h in range(heads)]
    grads = {}

    def block(h, b):
        rows = slice(b * QUERIES, (b + 1) * QUERIES)
        queries, cots = q[h, rows], do[h, rows]
        keys, values = window(parts[h][0], b), window(parts[h][1], b)
        s = nt(queries, keys)
        dp = nt(cots, values)
        yield
        s = s * (scale * LOG2E)
        s = jnp.concatenate([s[:, :NEAR] + bias[b], s[:, NEAR:]], 1)
        top = jnp.max(s, 1, keepdims=True)
        yield
        e = jnp.exp2(s - top)
        inverse = 1.0 / jnp.sum(e, 1, keepdims=True)
        yield
        p = e * inverse
        rounded = p.astype(BF)
        out = nn(rounded, values).astype(BF)
        dv = tn(rounded[:, :NEAR], cots)
        yield
        att[h, rows] = out
        delta = jnp.sum(out.astype(F32) * cots.astype(F32), 1, keepdims=True)
        ds = (p * (dp - delta) * scale).astype(BF)
        dqs = nn(ds, keys)
        dk = tn(ds[:, :NEAR], queries)
        yield
        dq[h, rows] = dqs.astype(BF)
        grads[h, b] = (dk, dv)

    live = [block(h, b) for h in range(heads) for b in range(BLOCKS)]
    while live:
        for g in list(live):
            try:
                next(g)
            except StopIteration:
                live.remove(g)

    step = BLOCK_ROWS * TILE_W
    for h in range(heads):
        for i in range(2):
            g = [grads[h, b][i] for b in range(BLOCKS)]
            c = [g[0][:step], g[0][step:mid] + g[1][:step], g[1][step:mid] + g[2][:step], g[2][step:mid]]
            c = jnp.concatenate(c, 0)
            gup[h, i] = c[:EDGE].astype(BF)
            own[h, i] = c[EDGE : EDGE + TOKENS].astype(own.dtype)
            gdn[h, i] = c[EDGE + TOKENS :].astype(BF)
            w = BLOCK_ROWS * RADIUS
            sides = []
            for j in range(2):
                s = [x[mid + j * half : mid + (j + 1) * half] for x in g]
                s = jnp.concatenate([s[0][:w], s[0][w:] + s[1][:w], s[1][w:] + s[2][:w], s[2][w:]], 0)
                sides.append(s.astype(BF))
            ga[h, i] = lax.select(even[1] == 1, sides[1], sides[0])
            gb[h, i] = lax.select(even[1] == 1, sides[0], sides[1])


def attend(chunk, even, q, do, kv, up, dn, far, sa, sb, bias, heads=2):
    _, t, d = q.shape
    h = sa.shape[2]
    steps = h // heads

    def spec(x, offset=0):
        return pl.BlockSpec((heads,) + x.shape[1:], lambda g: (g + offset,) + (0,) * (len(x.shape) - 1))

    def whole(x):
        return pl.BlockSpec(x.shape, lambda g: (0,) * len(x.shape))

    outs = [sds(h, t, d)] * 2 + [sds(h, 2, n, d) for n in (t, EDGE, EDGE, STRIP, STRIP)]
    flops = h * BLOCKS * QUERIES * (4 * (NEAR + far.shape[2]) + 2 * NEAR) * d * 2
    args = (q, do, kv, up, dn, far)
    return pl.pallas_call(
        functools.partial(attend_kernel, heads),
        grid=(steps,),
        in_specs=[spec(x, chunk * steps) for x in args] + [whole(x) for x in (sa, sb, bias)] + [SMEM],
        out_specs=[spec(x) for x in outs],
        out_shape=outs,
        scratch_shapes=[pltpu.VMEM((2, h, 2, STRIP, d), BF)],
        compiler_params=PARAMS,
        cost_estimate=pl.CostEstimate(flops=flops, bytes_accessed=12 << 20, transcendentals=0),
        name="attend",
    )(*args, sa, sb, bias, even)


def near_bias():
    position = lax.axis_index("seq")
    tiles_y = lax.axis_size("seq") // TILES_X
    shape = (BLOCKS, QUERIES, NEAR)
    b = lax.broadcasted_iota(jnp.int32, shape, 0)
    i = lax.broadcasted_iota(jnp.int32, shape, 1)
    k = lax.broadcasted_iota(jnp.int32, shape, 2)
    mid = WIN_ROWS * TILE_W
    half = WIN_ROWS * RADIUS
    k_row = jnp.where(k < mid, k // TILE_W, (k - mid) % half // RADIUS) - RADIUS
    side = jnp.where(k < mid + half, k % RADIUS - RADIUS, k % RADIUS + TILE_W)
    k_col = jnp.where(k < mid, k % TILE_W, side)
    seen = (jnp.abs(k_row - i // TILE_W) <= RADIUS) & (jnp.abs(k_col - i % TILE_W) <= RADIUS)
    row = position // TILES_X * TILE_H + b * BLOCK_ROWS + k_row
    col = position % TILES_X * TILE_W + k_col
    inside = (row >= 0) & (row < tiles_y * TILE_H) & (col >= 0) & (col < TILES_X * TILE_W)
    return jnp.where(seen & inside, 0.0, FLOOR).astype(F32)


def shards(fine_queries, fine_keys, fine_values, coarse_keys, coarse_values, out_grad):
    position = lax.axis_index("seq")
    even = jnp.stack([1 - position // TILES_X % 2, 1 - position % TILES_X % 2]).astype(jnp.int32)
    coarse = jnp.concatenate(widened(jnp.stack([coarse_keys[0], coarse_values[0]], 1), 4), 0)
    start = even[0] * (TOKENS - EDGE)
    rows = [
        jnp.stack([lax.dynamic_slice_in_dim(x[0], o, EDGE, 0) for x in (fine_keys, fine_values)], 1)
        for o in (start, TOKENS - EDGE - start)
    ]
    coarse, *rows = lax.optimization_barrier((coarse, *rows))
    row_a, row_b = (exchange(x, True, which) for which, x in enumerate(rows))
    coarse = jnp.concatenate(widened(coarse, 16), 0)
    coarse, fine_queries, out_grad, fine_keys, fine_values = lax.optimization_barrier(
        (coarse, fine_queries, out_grad, fine_keys, fine_values)
    )
    pieces = widened(coarse, 1)
    queries, cots = to_heads(fine_queries, out_grad)
    kv = pairs_to_heads(fine_keys, fine_values)
    bias = near_bias()
    row_a, row_b, kv, queries, cots, bias = lax.optimization_barrier((row_a, row_b, kv, queries, cots, bias))
    strips = sides(even, row_a, row_b, fine_keys[0], fine_values[0])
    side_a, side_b = ([exchange(x, False, which) for x in xs] for which, xs in enumerate(strips))
    up, dn = halo_to_heads(even, row_a, row_b)
    far = far_heads(pieces)
    att, dq, own, gup, gdn, from_a, from_b = ([] for _ in range(7))
    for c in range(CHUNKS):
        a, b, mine, u, n, ga, gb = attend(
            c, even, queries, cots, kv, up, dn, far, side_a[c], side_b[c], bias
        )
        from_a.append(exchange(ga, False, 0))
        from_b.append(exchange(gb, False, 1))
        for xs, x in ((att, a), (dq, b), (own, mine), (gup, u), (gdn, n)):
            xs.append(x)
    to_a, to_b = fold(even, gup, gdn, from_a, from_b)
    to_a, to_b = exchange(to_a, True, 0), exchange(to_b, True, 1)
    attended, query_grad = to_tokens(att, dq)
    dk, dv = premerge(even, own, from_a, from_b)
    key_grad, value_grad = finish(even, dk, dv, to_a, to_b)
    return (attended, query_grad, key_grad, value_grad)


def solution(mesh):
    spec = P("dp", "seq", "head", None)
    return jax.shard_map(
        shards, mesh=mesh, in_specs=(spec,) * 6, out_specs=(spec,) * 4, check_vma=False
    )
```

profile of v0, /device:TPU:6, one launch (start us, length us, event | category | flops | bytes accessed | tf_op | source)
XLA Modules:
  0.0 141.2 jit_solution(1123409149651894303)
XLA Ops:
  0.6 0.7 pad_maximum_fusion.4
  1.4 2.2 %collective-permute-start.2 = (bf16[4,2,16,128]{3,2,1,0:T(8,128)(2,1)S(1)}, bf16[4,2,16,128]{3,2,1,0:T(8,128)(2,1)S(1)}, u32[]{:S(2)}, u32[]{:S(2)}) collective-permute-start(bf16[4,2,16,128]{3,2,1,0:T(8,128)(2,1)S(1)} %pad_maximum_fusion.4), channel_id=1, source_target_pairs={{0,24},{2,26},{4,28},{6,30},{8,16},{10,18},{12,20},{14,22},{16,8},... | collective-permute-start | bytes 98312 | tf_op jit(solution)/shard_map/ppermute | solution.py:69
  3.6 0.7 collective-permute-start.1
  4.3 1.2 collective-permute-start
  5.6 1.4 dynamic-slice_bitcast_fusion
  7.0 0.0 copy-start.3
  7.0 0.0 copy-start.4
  7.0 0.8 pad_maximum_fusion.1
  7.8 0.8 pad_maximum_fusion
  8.7 0.0 collective-permute-done.2
  8.7 0.3 collective-permute-done.1
  9.0 0.0 collective-permute-done
  9.0 4.4 %collective-permute-start.7 = (bf16[16,2,16,128]{3,2,1,0:T(8,128)(2,1)S(1)}, bf16[16,2,16,128]{3,2,1,0:T(8,128)(2,1)S(1)}, u32[]{:S(2)}, u32[]{:S(2)}) collective-permute-start(bf16[16,2,16,128]{3,2,1,0:T(8,128)(2,1)S(1)} %pad_maximum_fusion.3), channel_id=1, source_target_pairs={{0,96},{2,98},{4,100},{6,102},{8,104},{10,106},{12,108},{14,110},{... | collective-permute-start | bytes 393224 | tf_op jit(solution)/shard_map/ppermute | solution.py:69
  13.4 0.0 collective-permute-start.6
  13.4 0.7 collective-permute-start.5
  14.1 1.4 %collective-permute-start.3 = (bf16[64,2,16,128]{3,2,1,0:T(8,128)(2,1)}, bf16[64,2,16,128]{3,2,1,0:T(8,128)(2,1)}, u32[]{:S(2)}, u32[]{:S(2)}) collective-permute-start(bf16[64,2,16,128]{3,2,1,0:T(8,128)(2,1)} %pad_maximum_fusion), channel_id=1, source_target_pairs={{0,16},{2,18},{4,20},{6,22},{8,24},{10,26},{12,28},{14,30},{16,0},... | collective-permute-start | bytes 1572872 | tf_op jit(solution)/shard_map/ppermute | solution.py:61
  15.5 2.9 %collective-permute-start.4 = (bf16[64,2,16,128]{3,2,1,0:T(8,128)(2,1)}, bf16[64,2,16,128]{3,2,1,0:T(8,128)(2,1)}, u32[]{:S(2)}, u32[]{:S(2)}) collective-permute-start(bf16[64,2,16,128]{3,2,1,0:T(8,128)(2,1)} %pad_maximum_fusion.1), channel_id=1, source_target_pairs={{0,2},{2,0},{4,6},{6,4},{8,10},{10,8},{12,14},{14,12},{16,32},{18,... | collective-permute-start | bytes 1572872 | tf_op jit(solution)/shard_map/ppermute | solution.py:61
  18.4 0.6 pad_add_fusion.even
  19.0 0.0 collective-permute-done.7
  19.0 4.2 %collective-permute-done.6 = bf16[16,2,16,128]{3,2,1,0:T(8,128)(2,1)S(1)} collective-permute-done((bf16[16,2,16,128]{3,2,1,0:T(8,128)(2,1)S(1)}, bf16[16,2,16,128]{3,2,1,0:T(8,128)(2,1)S(1)}, u32[]{:S(2)}, u32[]{:S(2)}) %collective-permute-start.6) | collective-permute-done | bytes 131104 | tf_op jit(solution)/shard_map/ppermute | solution.py:69
  23.2 0.0 collective-permute-done.5
  23.2 0.1 pad_maximum_fusion.2.refs_0_
  23.3 3.1 %collective-permute-start.10 = (bf16[64,2,16,128]{3,2,1,0:T(8,128)(2,1)S(1)}, bf16[64,2,16,128]{3,2,1,0:T(8,128)(2,1)}, u32[]{:S(2)}, u32[]{:S(2)}) collective-permute-start(bf16[64,2,16,128]{3,2,1,0:T(8,128)(2,1)S(1)} %pad_maximum_fusion.2.refs_0_), channel_id=1, source_target_pairs={{0,6},{2,4},{4,2},{6,0},{8,14},{10,12},{12,10},{14,8},{16,22},{18,... | collective-permute-start | bytes 1572872 | tf_op jit(solution)/shard_map/ppermute | solution.py:69
  26.4 0.6 collective-permute-start.9
  27.0 1.1 fusion.16.bias
  28.1 0.5 collective-permute-start.8
  28.5 4.7 %pairs_to_heads.1.kv = bf16[16,2,384,128]{3,2,1,0:T(8,128)(2,1)} custom-call(bf16[1,384,16,128]{3,2,1,0:T(8,128)(2,1)} %k, bf16[1,384,16,128]{3,2,1,0:T(8,128)(2,1)} %v), custom_call_target="tpu_custom_call" | custom-call | tf_op jit(solution)/shard_map/pairs_to_heads/pallas_call | solution.py:81
  33.2 0.0 copy-done
  33.2 4.2 %to_heads.1 = (bf16[16,384,128]{2,1,0:T(8,128)(2,1)}, bf16[16,384,128]{2,1,0:T(8,128)(2,1)}) custom-call(bf16[1,384,16,128]{3,2,1,0:T(8,128)(2,1)} %x, bf16[1,384,16,128]{3,2,1,0:T(8,128)(2,1)} %y), custom_call_target="tpu_custom_call" | custom-call | tf_op jit(solution)/shard_map/to_heads/pallas_call | solution.py:96
  37.4 2.0 %collective-permute-done.3.x.a = bf16[64,2,16,128]{3,2,1,0:T(8,128)(2,1)} collective-permute-done((bf16[64,2,16,128]{3,2,1,0:T(8,128)(2,1)}, bf16[64,2,16,128]{3,2,1,0:T(8,128)(2,1)}, u32[]{:S(2)}, u32[]{:S(2)}) %collective-permute-start.3) | collective-permute-done | bytes 524320 | tf_op jit(solution)/shard_map/ppermute | solution.py:61
  39.4 0.0 collective-permute-done.4.y.b
  39.4 4.0 %sides.1 = (bf16[128,2,8,128]{3,2,1,0:T(8,128)(2,1)}, bf16[128,2,8,128]{3,2,1,0:T(8,128)(2,1)}, bf16[128,2,8,128]{3,2,1,0:T(8,128)(2,1)}, bf16[128,2,8,128]{3,2,1,0:T(8,128)(2,1)}) custom-call(s32[2]{0:T(128)} %pad_add_fusion.even, bf16[64,2,16,128]{3,2,1,0:T(8,128)(2,1)} %collective-permute-done.3.x.a, bf16[64,2,16,128]{3,2,1,0:T(8,128)(2,1)} %collective-permute-done.4.y.b, ...), custom_call_target="tpu_custom_call" | custom-call | tf_op jit(solution)/shard_map/sides/pallas_call | solution.py:173
  43.5 1.6 %collective-permute-start.13 = (bf16[128,2,8,128]{3,2,1,0:T(8,128)(2,1)}, bf16[128,2,8,128]{3,2,1,0:T(8,128)(2,1)}, u32[]{:S(2)}, u32[]{:S(2)}) collective-permute-start(bf16[128,2,8,128]{3,2,1,0:T(8,128)(2,1)} %get-tuple-element.69), channel_id=1, source_target_pairs={{0,2},{2,0},{4,6},{6,4},{8,10},{10,8},{12,14},{14,12},{16,18},{18,... | collective-permute-start | bytes 1572872 | tf_op jit(solution)/shard_map/ppermute | solution.py:61
  45.0 2.4 %collective-permute-start.14 = (bf16[128,2,8,128]{3,2,1,0:T(8,128)(2,1)}, bf16[128,2,8,128]{3,2,1,0:T(8,128)(2,1)}, u32[]{:S(2)}, u32[]{:S(2)}) collective-permute-start(bf16[128,2,8,128]{3,2,1,0:T(8,128)(2,1)} %get-tuple-element.70), channel_id=1, source_target_pairs={{0,32},{2,4},{4,2},{6,8},{8,6},{10,12},{12,10},{14,46},{16,48},{18... | collective-permute-start | bytes 1572872 | tf_op jit(solution)/shard_map/ppermute | solution.py:61
  47.5 12.4 %collective-permute-done.10.refs_3_ = bf16[64,2,16,128]{3,2,1,0:T(8,128)(2,1)} collective-permute-done((bf16[64,2,16,128]{3,2,1,0:T(8,128)(2,1)S(1)}, bf16[64,2,16,128]{3,2,1,0:T(8,128)(2,1)}, u32[]{:S(2)}, u32[]{:S(2)}) %collective-permute-start.10) | collective-permute-done | bytes 524320 | tf_op jit(solution)/shard_map/ppermute | solution.py:69
  59.9 0.0 collective-permute-start.11
  59.9 0.0 collective-permute-done.9.refs_2_
  59.9 3.2 %collective-permute-start.12 = (bf16[128,2,8,128]{3,2,1,0:T(8,128)(2,1)}, bf16[128,2,8,128]{3,2,1,0:T(8,128)(2,1)}, u32[]{:S(2)}, u32[]{:S(2)}) collective-permute-start(bf16[128,2,8,128]{3,2,1,0:T(8,128)(2,1)} %get-tuple-element.66), channel_id=1, source_target_pairs={{0,32},{2,4},{4,2},{6,8},{8,6},{10,12},{12,10},{14,46},{16,48},{18... | collective-permute-start | bytes 1572872 | tf_op jit(solution)/shard_map/ppermute | solution.py:61
  63.1 2.4 %halo_to_heads.1 = (bf16[16,2,64,128]{3,2,1,0:T(8,128)(2,1)}, bf16[16,2,64,128]{3,2,1,0:T(8,128)(2,1)}) custom-call(s32[2]{0:T(128)} %pad_add_fusion.even, bf16[64,2,16,128]{3,2,1,0:T(8,128)(2,1)} %collective-permute-done.3.x.a, bf16[64,2,16,128]{3,2,1,0:T(8,128)(2,1)} %collective-permute-done.4.y.b), custom_call_target="tpu_custom_call" | custom-call | tf_op jit(solution)/shard_map/halo_to_heads/pallas_call | solution.py:115
  65.5 0.0 collective-permute-done.8.refs_1_
  65.5 2.8 %far_heads.1.far = bf16[16,2,256,128]{3,2,1,0:T(8,128)(2,1)} custom-call(bf16[64,2,16,128]{3,2,1,0:T(8,128)(2,1)} %copy-done, bf16[64,2,16,128]{3,2,1,0:T(8,128)(2,1)} %collective-permute-done.8.refs_1_, bf16[64,2,16,128]{3,2,1,0:T(8,128)(2,1)} %collective-permute-done.9.refs_2_, bf16[64,2,16,128]{3,2,1,0:T(8,128)(2,1)} %collective-permute-done.10.refs_3_), custom_call_target="tpu_custom_call" | custom-call | tf_op jit(solution)/shard_map/far_heads/pallas_call | solution.py:136
  68.3 0.0 collective-permute-done.13.sa
  68.3 0.0 collective-permute-done.14.sb
  68.3 11.9 %attend.3 = (bf16[8,384,128]{2,1,0:T(8,128)(2,1)}, bf16[8,384,128]{2,1,0:T(8,128)(2,1)}, bf16[8,2,384,128]{3,2,1,0:T(8,128)(2,1)}, bf16[8,2,64,128]{3,2,1,0:T(8,...) custom-call(bf16[16,384,128]{2,1,0:T(8,128)(2,1)} %get-tuple-element., ...), custom_call_target="tpu_custom_call" | custom-call | flops 2617245696 | bytes 12582912 | tf_op jit(solution)/shard_map/attend/pallas_call | solution.py:399
  80.2 0.1 collective-permute-start.16
  80.3 2.0 %collective-permute-start.18 = (bf16[8,2,128,128]{3,2,1,0:T(8,128)(2,1)}, bf16[8,2,128,128]{3,2,1,0:T(8,128)(2,1)}, u32[]{:S(2)}, u32[]{:S(2)}) collective-permute-start(bf16[8,2,128,128]{3,2,1,0:T(8,128)(2,1)} %get-tuple-element.81), channel_id=1, source_target_pairs={{0,32},{2,4},{4,2},{6,8},{8,6},{10,12},{12,10},{14,46},{16,48},{18... | collective-permute-start | bytes 1572872 | tf_op jit(solution)/shard_map/ppermute | solution.py:61
  82.3 0.0 collective-permute-done.11.sa
  82.3 0.0 collective-permute-done.12.sb
  82.4 11.9 %attend.2 = (bf16[8,384,128]{2,1,0:T(8,128)(2,1)}, bf16[8,384,128]{2,1,0:T(8,128)(2,1)}, bf16[8,2,384,128]{3,2,1,0:T(8,128)(2,1)}, bf16[8,2,64,128]{3,2,1,0:T(8,...) custom-call(bf16[16,384,128]{2,1,0:T(8,128)(2,1)} %get-tuple-element., ...), custom_call_target="tpu_custom_call" | custom-call | flops 2617245696 | bytes 12582912 | tf_op jit(solution)/shard_map/attend/pallas_call | solution.py:399
  94.2 0.1 collective-permute-start.15
  94.3 4.1 %collective-permute-start.17 = (bf16[8,2,128,128]{3,2,1,0:T(8,128)(2,1)}, bf16[8,2,128,128]{3,2,1,0:T(8,128)(2,1)}, u32[]{:S(2)}, u32[]{:S(2)}) collective-permute-start(bf16[8,2,128,128]{3,2,1,0:T(8,128)(2,1)} %get-tuple-element.80), channel_id=1, source_target_pairs={{0,32},{2,4},{4,2},{6,8},{8,6},{10,12},{12,10},{14,46},{16,48},{18... | collective-permute-start | bytes 1572872 | tf_op jit(solution)/shard_map/ppermute | solution.py:61
  98.4 0.0 collective-permute-done.16.refs_3_.refs_5_
  98.4 0.0 collective-permute-done.18.refs_5_.refs_7_
  98.5 8.7 %collective-permute-done.15.refs_2_.refs_4_ = bf16[8,2,128,128]{3,2,1,0:T(8,128)(2,1)} collective-permute-done((bf16[8,2,128,128]{3,2,1,0:T(8,128)(2,1)}, bf16[8,2,128,128]{3,2,1,0:T(8,128)(2,1)}, u32[]{:S(2)}, u32[]{:S(2)}) %collective-permute-start.15) | collective-permute-done | bytes 524320 | tf_op jit(solution)/shard_map/ppermute | solution.py:61
  107.1 2.2 %collective-permute-done.17.refs_4_.refs_6_ = bf16[8,2,128,128]{3,2,1,0:T(8,128)(2,1)} collective-permute-done((bf16[8,2,128,128]{3,2,1,0:T(8,128)(2,1)}, bf16[8,2,128,128]{3,2,1,0:T(8,128)(2,1)}, u32[]{:S(2)}, u32[]{:S(2)}) %collective-permute-start.17) | collective-permute-done | bytes 524320 | tf_op jit(solution)/shard_map/ppermute | solution.py:61
  109.4 3.2 %fold.1 = (bf16[64,2,16,128]{3,2,1,0:T(8,128)(2,1)}, bf16[64,2,16,128]{3,2,1,0:T(8,128)(2,1)}) custom-call(s32[2]{0:T(128)} %pad_add_fusion.even, bf16[8,2,64,128]{3,2,1,0:T(8,128)(2,1)} %get-tuple-element.84.refs_0_, bf16[8,2,64,128]{3,2,1,0:T(8,128)(2,1)} %get-tuple-element.85.refs_1_, bf16[8,2,64,128]{3,2,1,0:T(8,128)(2,1)} %get-tuple-element.86.refs_2_, ...), custom_call_target="tpu_custom_call" | custom-call | tf_op jit(solution)/shard_map/fold/pallas_call | solution.py:232
  112.6 0.1 collective-permute-start.19
  112.7 7.0 %collective-permute-start.20 = (bf16[64,2,16,128]{3,2,1,0:T(8,128)(2,1)}, bf16[64,2,16,128]{3,2,1,0:T(8,128)(2,1)}, u32[]{:S(2)}, u32[]{:S(2)}) collective-permute-start(bf16[64,2,16,128]{3,2,1,0:T(8,128)(2,1)} %get-tuple-element.89), channel_id=1, source_target_pairs={{0,2},{2,0},{4,6},{6,4},{8,10},{10,8},{12,14},{14,12},{16,32},{18,... | collective-permute-start | bytes 1572872 | tf_op jit(solution)/shard_map/ppermute | solution.py:61
  119.7 4.0 %to_tokens.1 = (bf16[1,384,16,128]{3,2,1,0:T(8,128)(2,1)}, bf16[1,384,16,128]{3,2,1,0:T(8,128)(2,1)}) custom-call(bf16[8,384,128]{2,1,0:T(8,128)(2,1)} %get-tuple-element.68.refs_0_, bf16[8,384,128]{2,1,0:T(8,128)(2,1)} %get-tuple-element.71.refs_1_, bf16[8,384,128]{2,1,0:T(8,128)(2,1)} %get-tuple-element.72.refs_2_, ...), custom_call_target="tpu_custom_call" | custom-call | tf_op jit(solution)/shard_map/to_tokens/pallas_call | solution.py:197
  123.6 5.7 %premerge.1 = (bf16[1,384,16,128]{3,2,1,0:T(8,128)(2,1)}, bf16[1,384,16,128]{3,2,1,0:T(8,128)(2,1)}) custom-call(s32[2]{0:T(128)} %pad_add_fusion.even, bf16[8,2,384,128]{3,2,1,0:T(8,128)(2,1)} %get-tuple-element.76.refs_0_, bf16[8,2,384,128]{3,2,1,0:T(8,128)(2,1)} %get-tuple-element.77.refs_1_, ...), custom_call_target="tpu_custom_call" | custom-call | tf_op jit(solution)/shard_map/premerge/pallas_call | solution.py:266
  129.3 7.9 %collective-permute-done.19.from_a = bf16[64,2,16,128]{3,2,1,0:T(8,128)(2,1)S(1)} collective-permute-done((bf16[64,2,16,128]{3,2,1,0:T(8,128)(2,1)}, bf16[64,2,16,128]{3,2,1,0:T(8,128)(2,1)S(1)}, u32[]{:S(2)}, u32[]{:S(2)}) %collective-permute-start.19) | collective-permute-done | bytes 524320 | tf_op jit(solution)/shard_map/ppermute | solution.py:61
  137.2 0.0 collective-permute-done.20.from_b
  137.2 0.8 copy-done.2
  138.1 3.2 %finish.1 = (bf16[1,384,16,128]{3,2,1,0:T(8,128)(2,1)}, bf16[1,384,16,128]{3,2,1,0:T(8,128)(2,1)}) custom-call(s32[2]{0:T(128)} %pad_add_fusion.even, bf16[1,384,16,128]{3,2,1,0:T(8,128)(2,1)} %get-tuple-element.82.dk, bf16[1,384,16,128]{3,2,1,0:T(8,128)(2,1)} %get-tuple-element.83.dv, ...), custom_call_target="tpu_custom_call", output_to_operand_aliasing={{0}: (1, {}), {1}: (2, {})} | custom-call | tf_op jit(solution)/shard_map/finish/pallas_call | solution.py:289
  (18 shorter events, 0.1 us)
Async XLA Ops:
  1.4 7.3 %collective-permute-start.2 = (bf16[4,2,16,128]{3,2,1,0:T(8,128)(2,1)S(1)}, bf16[4,2,16,128]{3,2,1,0:T(8,128)(2,1)S(1)}, u32[]{:S(2)}, u32[]{:S(2)}) collective-permute-start(bf16[4,2,16,128]{3,2,1,0:T(8,128)(2,1)S(1)} %pad_maximum_fusion.4), channel_id=1, source_target_pairs={{0,24},{2,26},{4,28},{6,30},{8,16},{10,18},{12,20},{14,22},{16,8},... | collective-permute-start | bytes 98312 | tf_op jit(solution)/shard_map/ppermute | solution.py:69
  3.6 5.4 %collective-permute-start.1 = (bf16[4,2,16,128]{3,2,1,0:T(8,128)(2,1)S(1)}, bf16[4,2,16,128]{3,2,1,0:T(8,128)(2,1)S(1)}, u32[]{:S(2)}, u32[]{:S(2)}) collective-permute-start(bf16[4,2,16,128]{3,2,1,0:T(8,128)(2,1)S(1)} %pad_maximum_fusion.4), channel_id=1, source_target_pairs={{0,16},{2,18},{4,20},{6,22},{8,24},{10,26},{12,28},{14,30},{16,0},... | collective-permute-start | bytes 98312 | tf_op jit(solution)/shard_map/ppermute | solution.py:69
  4.3 4.7 %collective-permute-start = (bf16[4,2,16,128]{3,2,1,0:T(8,128)(2,1)S(1)}, bf16[4,2,16,128]{3,2,1,0:T(8,128)(2,1)S(1)}, u32[]{:S(2)}, u32[]{:S(2)}) collective-permute-start(bf16[4,2,16,128]{3,2,1,0:T(8,128)(2,1)S(1)} %pad_maximum_fusion.4), channel_id=1, source_target_pairs={{0,8},{2,10},{4,12},{6,14},{8,0},{10,2},{12,4},{14,6},{16,24},{18,... | collective-permute-start | bytes 98312 | tf_op jit(solution)/shard_map/ppermute | solution.py:69
  7.0 2.1 %copy-start.3 = (bf16[1,4,16,128]{3,2,1,0:T(8,128)(2,1)S(1)}, bf16[1,4,16,128]{3,2,1,0:T(8,128)(2,1)}, u32[]{:S(2)}) copy-start(bf16[1,4,16,128]{3,2,1,0:T(8,128)(2,1)} %param.10) | copy-start | bytes 49156
  7.0 2.0 %copy-start.4 = (bf16[1,4,16,128]{3,2,1,0:T(8,128)(2,1)S(1)}, bf16[1,4,16,128]{3,2,1,0:T(8,128)(2,1)}, u32[]{:S(2)}) copy-start(bf16[1,4,16,128]{3,2,1,0:T(8,128)(2,1)} %param.9) | copy-start | bytes 49156
  9.0 10.0 %collective-permute-start.7 = (bf16[16,2,16,128]{3,2,1,0:T(8,128)(2,1)S(1)}, bf16[16,2,16,128]{3,2,1,0:T(8,128)(2,1)S(1)}, u32[]{:S(2)}, u32[]{:S(2)}) collective-permute-start(bf16[16,2,16,128]{3,2,1,0:T(8,128)(2,1)S(1)} %pad_maximum_fusion.3), channel_id=1, source_target_pairs={{0,96},{2,98},{4,100},{6,102},{8,104},{10,106},{12,108},{14,110},{... | collective-permute-start | bytes 393224 | tf_op jit(solution)/shard_map/ppermute | solution.py:69
  13.4 9.7 %collective-permute-start.6 = (bf16[16,2,16,128]{3,2,1,0:T(8,128)(2,1)S(1)}, bf16[16,2,16,128]{3,2,1,0:T(8,128)(2,1)S(1)}, u32[]{:S(2)}, u32[]{:S(2)}) collective-permute-start(bf16[16,2,16,128]{3,2,1,0:T(8,128)(2,1)S(1)} %pad_maximum_fusion.3), channel_id=1, source_target_pairs={{0,64},{2,66},{4,68},{6,70},{8,72},{10,74},{12,76},{14,78},{16,80}... | collective-permute-start | bytes 393224 | tf_op jit(solution)/shard_map/ppermute | solution.py:69
  13.4 9.7 %collective-permute-start.5 = (bf16[16,2,16,128]{3,2,1,0:T(8,128)(2,1)S(1)}, bf16[16,2,16,128]{3,2,1,0:T(8,128)(2,1)S(1)}, u32[]{:S(2)}, u32[]{:S(2)}) collective-permute-start(bf16[16,2,16,128]{3,2,1,0:T(8,128)(2,1)S(1)} %pad_maximum_fusion.3), channel_id=1, source_target_pairs={{0,32},{2,34},{4,36},{6,38},{8,40},{10,42},{12,44},{14,46},{16,48}... | collective-permute-start | bytes 393224 | tf_op jit(solution)/shard_map/ppermute | solution.py:69
  14.1 25.3 %collective-permute-start.3 = (bf16[64,2,16,128]{3,2,1,0:T(8,128)(2,1)}, bf16[64,2,16,128]{3,2,1,0:T(8,128)(2,1)}, u32[]{:S(2)}, u32[]{:S(2)}) collective-permute-start(bf16[64,2,16,128]{3,2,1,0:T(8,128)(2,1)} %pad_maximum_fusion), channel_id=1, source_target_pairs={{0,16},{2,18},{4,20},{6,22},{8,24},{10,26},{12,28},{14,30},{16,0},... | collective-permute-start | bytes 1572872 | tf_op jit(solution)/shard_map/ppermute | solution.py:61
  15.5 23.9 %collective-permute-start.4 = (bf16[64,2,16,128]{3,2,1,0:T(8,128)(2,1)}, bf16[64,2,16,128]{3,2,1,0:T(8,128)(2,1)}, u32[]{:S(2)}, u32[]{:S(2)}) collective-permute-start(bf16[64,2,16,128]{3,2,1,0:T(8,128)(2,1)} %pad_maximum_fusion.1), channel_id=1, source_target_pairs={{0,2},{2,0},{4,6},{6,4},{8,10},{10,8},{12,14},{14,12},{16,32},{18,... | collective-permute-start | bytes 1572872 | tf_op jit(solution)/shard_map/ppermute | solution.py:61
  23.2 10.0 %copy-start = (bf16[64,2,16,128]{3,2,1,0:T(8,128)(2,1)}, bf16[64,2,16,128]{3,2,1,0:T(8,128)(2,1)S(1)}, u32[]{:S(2)}) copy-start(bf16[64,2,16,128]{3,2,1,0:T(8,128)(2,1)S(1)} %pad_maximum_fusion.2.refs_0_) | copy-start | bytes 1572868
  23.3 36.6 %collective-permute-start.10 = (bf16[64,2,16,128]{3,2,1,0:T(8,128)(2,1)S(1)}, bf16[64,2,16,128]{3,2,1,0:T(8,128)(2,1)}, u32[]{:S(2)}, u32[]{:S(2)}) collective-permute-start(bf16[64,2,16,128]{3,2,1,0:T(8,128)(2,1)S(1)} %pad_maximum_fusion.2.refs_0_), channel_id=1, source_target_pairs={{0,6},{2,4},{4,2},{6,0},{8,14},{10,12},{12,10},{14,8},{16,22},{18,... | collective-permute-start | bytes 1572872 | tf_op jit(solution)/shard_map/ppermute | solution.py:69
  26.4 33.5 %collective-permute-start.9 = (bf16[64,2,16,128]{3,2,1,0:T(8,128)(2,1)S(1)}, bf16[64,2,16,128]{3,2,1,0:T(8,128)(2,1)}, u32[]{:S(2)}, u32[]{:S(2)}) collective-permute-start(bf16[64,2,16,128]{3,2,1,0:T(8,128)(2,1)S(1)} %pad_maximum_fusion.2.refs_0_), channel_id=1, source_target_pairs={{0,4},{2,6},{4,0},{6,2},{8,12},{10,14},{12,8},{14,10},{16,20},{18,... | collective-permute-start | bytes 1572872 | tf_op jit(solution)/shard_map/ppermute | solution.py:69
  28.1 37.4 %collective-permute-start.8 = (bf16[64,2,16,128]{3,2,1,0:T(8,128)(2,1)S(1)}, bf16[64,2,16,128]{3,2,1,0:T(8,128)(2,1)}, u32[]{:S(2)}, u32[]{:S(2)}) collective-permute-start(bf16[64,2,16,128]{3,2,1,0:T(8,128)(2,1)S(1)} %pad_maximum_fusion.2.refs_0_), channel_id=1, source_target_pairs={{0,2},{2,0},{4,6},{6,4},{8,10},{10,8},{12,14},{14,12},{16,18},{18,... | collective-permute-start | bytes 1572872 | tf_op jit(solution)/shard_map/ppermute | solution.py:69
  43.5 24.9 %collective-permute-start.13 = (bf16[128,2,8,128]{3,2,1,0:T(8,128)(2,1)}, bf16[128,2,8,128]{3,2,1,0:T(8,128)(2,1)}, u32[]{:S(2)}, u32[]{:S(2)}) collective-permute-start(bf16[128,2,8,128]{3,2,1,0:T(8,128)(2,1)} %get-tuple-element.69), channel_id=1, source_target_pairs={{0,2},{2,0},{4,6},{6,4},{8,10},{10,8},{12,14},{14,12},{16,18},{18,... | collective-permute-start | bytes 1572872 | tf_op jit(solution)/shard_map/ppermute | solution.py:61
  45.0 23.3 %collective-permute-start.14 = (bf16[128,2,8,128]{3,2,1,0:T(8,128)(2,1)}, bf16[128,2,8,128]{3,2,1,0:T(8,128)(2,1)}, u32[]{:S(2)}, u32[]{:S(2)}) collective-permute-start(bf16[128,2,8,128]{3,2,1,0:T(8,128)(2,1)} %get-tuple-element.70), channel_id=1, source_target_pairs={{0,32},{2,4},{4,2},{6,8},{8,6},{10,12},{12,10},{14,46},{16,48},{18... | collective-permute-start | bytes 1572872 | tf_op jit(solution)/shard_map/ppermute | solution.py:61
  59.9 22.5 %collective-permute-start.11 = (bf16[128,2,8,128]{3,2,1,0:T(8,128)(2,1)}, bf16[128,2,8,128]{3,2,1,0:T(8,128)(2,1)}, u32[]{:S(2)}, u32[]{:S(2)}) collective-permute-start(bf16[128,2,8,128]{3,2,1,0:T(8,128)(2,1)} %get-tuple-element.65), channel_id=1, source_target_pairs={{0,2},{2,0},{4,6},{6,4},{8,10},{10,8},{12,14},{14,12},{16,18},{18,... | collective-permute-start | bytes 1572872 | tf_op jit(solution)/shard_map/ppermute | solution.py:61
  59.9 22.5 %collective-permute-start.12 = (bf16[128,2,8,128]{3,2,1,0:T(8,128)(2,1)}, bf16[128,2,8,128]{3,2,1,0:T(8,128)(2,1)}, u32[]{:S(2)}, u32[]{:S(2)}) collective-permute-start(bf16[128,2,8,128]{3,2,1,0:T(8,128)(2,1)} %get-tuple-element.66), channel_id=1, source_target_pairs={{0,32},{2,4},{4,2},{6,8},{8,6},{10,12},{12,10},{14,46},{16,48},{18... | collective-permute-start | bytes 1572872 | tf_op jit(solution)/shard_map/ppermute | solution.py:61
  80.2 18.2 %collective-permute-start.16 = (bf16[8,2,128,128]{3,2,1,0:T(8,128)(2,1)}, bf16[8,2,128,128]{3,2,1,0:T(8,128)(2,1)S(1)}, u32[]{:S(2)}, u32[]{:S(2)}) collective-permute-start(bf16[8,2,128,128]{3,2,1,0:T(8,128)(2,1)} %get-tuple-element.79), channel_id=1, source_target_pairs={{0,2},{2,0},{4,6},{6,4},{8,10},{10,8},{12,14},{14,12},{16,18},{18,... | collective-permute-start | bytes 1572872 | tf_op jit(solution)/shard_map/ppermute | solution.py:61
  80.3 18.1 %collective-permute-start.18 = (bf16[8,2,128,128]{3,2,1,0:T(8,128)(2,1)}, bf16[8,2,128,128]{3,2,1,0:T(8,128)(2,1)}, u32[]{:S(2)}, u32[]{:S(2)}) collective-permute-start(bf16[8,2,128,128]{3,2,1,0:T(8,128)(2,1)} %get-tuple-element.81), channel_id=1, source_target_pairs={{0,32},{2,4},{4,2},{6,8},{8,6},{10,12},{12,10},{14,46},{16,48},{18... | collective-permute-start | bytes 1572872 | tf_op jit(solution)/shard_map/ppermute | solution.py:61
  94.2 12.9 %collective-permute-start.15 = (bf16[8,2,128,128]{3,2,1,0:T(8,128)(2,1)}, bf16[8,2,128,128]{3,2,1,0:T(8,128)(2,1)}, u32[]{:S(2)}, u32[]{:S(2)}) collective-permute-start(bf16[8,2,128,128]{3,2,1,0:T(8,128)(2,1)} %get-tuple-element.78), channel_id=1, source_target_pairs={{0,2},{2,0},{4,6},{6,4},{8,10},{10,8},{12,14},{14,12},{16,18},{18,... | collective-permute-start | bytes 1572872 | tf_op jit(solution)/shard_map/ppermute | solution.py:61
  94.3 15.0 %collective-permute-start.17 = (bf16[8,2,128,128]{3,2,1,0:T(8,128)(2,1)}, bf16[8,2,128,128]{3,2,1,0:T(8,128)(2,1)}, u32[]{:S(2)}, u32[]{:S(2)}) collective-permute-start(bf16[8,2,128,128]{3,2,1,0:T(8,128)(2,1)} %get-tuple-element.80), channel_id=1, source_target_pairs={{0,32},{2,4},{4,2},{6,8},{8,6},{10,12},{12,10},{14,46},{16,48},{18... | collective-permute-start | bytes 1572872 | tf_op jit(solution)/shard_map/ppermute | solution.py:61
  98.4 10.9 %copy-start.1 = (bf16[8,2,128,128]{3,2,1,0:T(8,128)(2,1)}, bf16[8,2,128,128]{3,2,1,0:T(8,128)(2,1)S(1)}, u32[]{:S(2)}) copy-start(bf16[8,2,128,128]{3,2,1,0:T(8,128)(2,1)S(1)} %collective-permute-done.16.refs_3_.refs_5_) | copy-start | bytes 1572868
  112.6 24.6 %collective-permute-start.19 = (bf16[64,2,16,128]{3,2,1,0:T(8,128)(2,1)}, bf16[64,2,16,128]{3,2,1,0:T(8,128)(2,1)S(1)}, u32[]{:S(2)}, u32[]{:S(2)}) collective-permute-start(bf16[64,2,16,128]{3,2,1,0:T(8,128)(2,1)} %get-tuple-element.88), channel_id=1, source_target_pairs={{0,16},{2,18},{4,20},{6,22},{8,24},{10,26},{12,28},{14,30},{16,0},... | collective-permute-start | bytes 1572872 | tf_op jit(solution)/shard_map/ppermute | solution.py:61
  112.7 24.5 %collective-permute-start.20 = (bf16[64,2,16,128]{3,2,1,0:T(8,128)(2,1)}, bf16[64,2,16,128]{3,2,1,0:T(8,128)(2,1)}, u32[]{:S(2)}, u32[]{:S(2)}) collective-permute-start(bf16[64,2,16,128]{3,2,1,0:T(8,128)(2,1)} %get-tuple-element.89), channel_id=1, source_target_pairs={{0,2},{2,0},{4,6},{6,4},{8,10},{10,8},{12,14},{14,12},{16,32},{18,... | collective-permute-start | bytes 1572872 | tf_op jit(solution)/shard_map/ppermute | solution.py:61
  137.2 0.8 copy-start.2
where the time goes:
time: 142 us; the launch traced here: 141 us
  Pallas kernels  57.9 us (41%)
  starting transfers between devices  38.3 us (27%)
  waiting for transfers between devices  37.8 us (27%)
  other arithmetic  4.2 us (3%)
  local copies, waits for them, and re-layouts  2.22 us (2%)
    ppermute x12, starting transfers between devices, exchange(): return lax.ppermute(value, 'seq', pairs)  25 us
    pallas_call x2, Pallas kernels, attend(): pl.pallas_call(functools.partial(attend_kernel, heads), grid=(steps,), in...  23.7 us
    ppermute x12, waiting for transfers between devices, exchange(): return lax.ppermute(value, 'seq', pairs)  20.9 us
    ppermute x9, waiting for transfers between devices, swapped(): return lax.ppermute(block, 'seq', pairs)  16.9 us
    ppermute x9, starting transfers between devices, swapped(): return lax.ppermute(block, 'seq', pairs)  13.3 us
    pallas_call x1, Pallas kernels, premerge(): pl.pallas_call(premerge_kernel, in_specs=[SMEM] + [VMEM] * (3 * CHUNKS),...  5.65 us
    pallas_call x1, Pallas kernels, pairs_to_heads(): pl.pallas_call(pairs_to_heads_kernel, out_shape=sds(h, 2, t, d), compiler...  4.7 us
    pallas_call x1, Pallas kernels, to_heads(): pl.pallas_call(to_heads_kernel, out_shape=[sds(h, t, d)] * 2, compiler_pa...  4.23 us
  transfers between devices with their start and end apart: 21, of which 7 were waited for; matrix products, arithmetic and copies ran while one was open for 3% of the time, Pallas kernels for 36%

commit v1 on v0

--- a/solution.py
+++ b/solution.py
@@ -55,7 +55,7 @@
         place, extent = (row, count // TILES_X) if rows else (col, TILES_X)
         target = ((place + which) ^ 1) - which
         if not 0 <= target < extent:
-            pairs.append((source, source ^ 1 if rows else source ^ (2 * TILES_X)))
+            pairs.append((source, source if rows else source ^ (2 * TILES_X)))
         else:
             pairs.append((source, target * TILES_X + col if rows else row * TILES_X + target))
     return lax.ppermute(value, "seq", pairs)

time: 142 us -> 142 us (level)
  starting transfers between devices: 38.3 us -> 42.3 us
  waiting for transfers between devices: 37.8 us -> 33.8 us
    ppermute x12, starting transfers between devices: 25 us -> 29 us  [exchange(): return lax.ppermute(value, 'seq', pairs)]
    ppermute x12, waiting for transfers between devices: 20.9 us -> 18.7 us  [exchange(): return lax.ppermute(value, 'seq', pairs)]
    ppermute x9, waiting for transfers between devices: 16.9 us -> 15 us  [swapped(): return lax.ppermute(block, 'seq', pairs)]
where the time goes in v1:
time: 142 us; the launch traced here: 141 us
  Pallas kernels  57.9 us (41%)
  starting transfers between devices  42.3 us (30%)
  waiting for transfers between devices  33.8 us (24%)
  other arithmetic  4.21 us (3%)
  local copies, waits for them, and re-layouts  2.22 us (2%)
    ppermute x12, starting transfers between devices, exchange(): return lax.ppermute(value, 'seq', pairs)  29 us
    pallas_call x2, Pallas kernels, attend(): pl.pallas_call(functools.partial(attend_kernel, heads), grid=(steps,), in...  23.7 us
    ppermute x12, waiting for transfers between devices, exchange(): return lax.ppermute(value, 'seq', pairs)  18.7 us
    ppermute x9, waiting for transfers between devices, swapped(): return lax.ppermute(block, 'seq', pairs)  15 us
    ppermute x9, starting transfers between devices, swapped(): return lax.ppermute(block, 'seq', pairs)  13.3 us
    pallas_call x1, Pallas kernels, premerge(): pl.pallas_call(premerge_kernel, in_specs=[SMEM] + [VMEM] * (3 * CHUNKS),...  5.65 us
    pallas_call x1, Pallas kernels, pairs_to_heads(): pl.pallas_call(pairs_to_heads_kernel, out_shape=sds(h, 2, t, d), compiler...  4.7 us
    pallas_call x1, Pallas kernels, to_heads(): pl.pallas_call(to_heads_kernel, out_shape=[sds(h, t, d)] * 2, compiler_pa...  4.23 us
  transfers between devices with their start and end apart: 21, of which 7 were waited for; matrix products, arithmetic and copies ran while one was open for 3% of the time, Pallas kernels for 36%

profile of v1, /device:TPU:6, one launch (start us, length us, event | category | flops | bytes accessed | tf_op | source)
XLA Modules:
  0.0 141.2 jit_solution(12309833716223334089)
XLA Ops:
  0.6 0.7 pad_maximum_fusion.4
  1.4 2.2 %collective-permute-start.2 = (bf16[4,2,16,128]{3,2,1,0:T(8,128)(2,1)S(1)}, bf16[4,2,16,128]{3,2,1,0:T(8,128)(2,1)S(1)}, u32[]{:S(2)}, u32[]{:S(2)}) collective-permute-start(bf16[4,2,16,128]{3,2,1,0:T(8,128)(2,1)S(1)} %pad_maximum_fusion.4), channel_id=1, source_target_pairs={{0,24},{2,26},{4,28},{6,30},{8,16},{10,18},{12,20},{14,22},{16,8},... | collective-permute-start | bytes 98312 | tf_op jit(solution)/shard_map/ppermute | solution.py:69
  3.6 0.7 collective-permute-start.1
  4.3 1.2 collective-permute-start
  5.6 1.4 dynamic-slice_bitcast_fusion
  7.0 0.0 copy-start.3
  7.0 0.0 copy-start.4
  7.0 0.8 pad_maximum_fusion.1
  7.8 0.8 pad_maximum_fusion
  8.7 0.0 collective-permute-done.2
  8.7 0.3 collective-permute-done.1
  9.0 0.0 collective-permute-done
  9.0 4.4 %collective-permute-start.7 = (bf16[16,2,16,128]{3,2,1,0:T(8,128)(2,1)S(1)}, bf16[16,2,16,128]{3,2,1,0:T(8,128)(2,1)S(1)}, u32[]{:S(2)}, u32[]{:S(2)}) collective-permute-start(bf16[16,2,16,128]{3,2,1,0:T(8,128)(2,1)S(1)} %pad_maximum_fusion.3), channel_id=1, source_target_pairs={{0,96},{2,98},{4,100},{6,102},{8,104},{10,106},{12,108},{14,110},{... | collective-permute-start | bytes 393224 | tf_op jit(solution)/shard_map/ppermute | solution.py:69
  13.4 0.0 collective-permute-start.6
  13.4 0.7 collective-permute-start.5
  14.1 1.4 %collective-permute-start.3 = (bf16[64,2,16,128]{3,2,1,0:T(8,128)(2,1)}, bf16[64,2,16,128]{3,2,1,0:T(8,128)(2,1)}, u32[]{:S(2)}, u32[]{:S(2)}) collective-permute-start(bf16[64,2,16,128]{3,2,1,0:T(8,128)(2,1)} %pad_maximum_fusion), channel_id=1, source_target_pairs={{0,16},{2,18},{4,20},{6,22},{8,24},{10,26},{12,28},{14,30},{16,0},... | collective-permute-start | bytes 1572872 | tf_op jit(solution)/shard_map/ppermute | solution.py:61
  15.5 4.8 %collective-permute-start.4 = (bf16[64,2,16,128]{3,2,1,0:T(8,128)(2,1)}, bf16[64,2,16,128]{3,2,1,0:T(8,128)(2,1)}, u32[]{:S(2)}, u32[]{:S(2)}) collective-permute-start(bf16[64,2,16,128]{3,2,1,0:T(8,128)(2,1)} %pad_maximum_fusion.1), channel_id=1, source_target_pairs={{0,0},{2,2},{4,4},{6,6},{8,8},{10,10},{12,12},{14,14},{16,32},{18,... | collective-permute-start | bytes 1572872 | tf_op jit(solution)/shard_map/ppermute | solution.py:61
  20.3 0.6 pad_add_fusion.even
  20.9 0.0 collective-permute-done.7
  20.9 2.3 %collective-permute-done.6 = bf16[16,2,16,128]{3,2,1,0:T(8,128)(2,1)S(1)} collective-permute-done((bf16[16,2,16,128]{3,2,1,0:T(8,128)(2,1)S(1)}, bf16[16,2,16,128]{3,2,1,0:T(8,128)(2,1)S(1)}, u32[]{:S(2)}, u32[]{:S(2)}) %collective-permute-start.6) | collective-permute-done | bytes 131104 | tf_op jit(solution)/shard_map/ppermute | solution.py:69
  23.2 0.0 collective-permute-done.5
  23.2 0.1 pad_maximum_fusion.2.refs_0_
  23.3 3.1 %collective-permute-start.10 = (bf16[64,2,16,128]{3,2,1,0:T(8,128)(2,1)S(1)}, bf16[64,2,16,128]{3,2,1,0:T(8,128)(2,1)}, u32[]{:S(2)}, u32[]{:S(2)}) collective-permute-start(bf16[64,2,16,128]{3,2,1,0:T(8,128)(2,1)S(1)} %pad_maximum_fusion.2.refs_0_), channel_id=1, source_target_pairs={{0,6},{2,4},{4,2},{6,0},{8,14},{10,12},{12,10},{14,8},{16,22},{18,... | collective-permute-start | bytes 1572872 | tf_op jit(solution)/shard_map/ppermute | solution.py:69
  26.4 0.6 collective-permute-start.9
  27.0 1.1 fusion.16.bias
  28.1 0.5 collective-permute-start.8
  28.5 4.7 %pairs_to_heads.1.kv = bf16[16,2,384,128]{3,2,1,0:T(8,128)(2,1)} custom-call(bf16[1,384,16,128]{3,2,1,0:T(8,128)(2,1)} %k, bf16[1,384,16,128]{3,2,1,0:T(8,128)(2,1)} %v), custom_call_target="tpu_custom_call" | custom-call | tf_op jit(solution)/shard_map/pairs_to_heads/pallas_call | solution.py:81
  33.2 0.0 copy-done
  33.2 4.2 %to_heads.1 = (bf16[16,384,128]{2,1,0:T(8,128)(2,1)}, bf16[16,384,128]{2,1,0:T(8,128)(2,1)}) custom-call(bf16[1,384,16,128]{3,2,1,0:T(8,128)(2,1)} %x, bf16[1,384,16,128]{3,2,1,0:T(8,128)(2,1)} %y), custom_call_target="tpu_custom_call" | custom-call | tf_op jit(solution)/shard_map/to_heads/pallas_call | solution.py:96
  37.4 2.0 %collective-permute-done.3.x.a = bf16[64,2,16,128]{3,2,1,0:T(8,128)(2,1)} collective-permute-done((bf16[64,2,16,128]{3,2,1,0:T(8,128)(2,1)}, bf16[64,2,16,128]{3,2,1,0:T(8,128)(2,1)}, u32[]{:S(2)}, u32[]{:S(2)}) %collective-permute-start.3) | collective-permute-done | bytes 524320 | tf_op jit(solution)/shard_map/ppermute | solution.py:61
  39.4 0.0 collective-permute-done.4.y.b
  39.4 4.0 %sides.1 = (bf16[128,2,8,128]{3,2,1,0:T(8,128)(2,1)}, bf16[128,2,8,128]{3,2,1,0:T(8,128)(2,1)}, bf16[128,2,8,128]{3,2,1,0:T(8,128)(2,1)}, bf16[128,2,8,128]{3,2,1,0:T(8,128)(2,1)}) custom-call(s32[2]{0:T(128)} %pad_add_fusion.even, bf16[64,2,16,128]{3,2,1,0:T(8,128)(2,1)} %collective-permute-done.3.x.a, bf16[64,2,16,128]{3,2,1,0:T(8,128)(2,1)} %collective-permute-done.4.y.b, ...), custom_call_target="tpu_custom_call" | custom-call | tf_op jit(solution)/shard_map/sides/pallas_call | solution.py:173
  43.5 1.6 %collective-permute-start.13 = (bf16[128,2,8,128]{3,2,1,0:T(8,128)(2,1)}, bf16[128,2,8,128]{3,2,1,0:T(8,128)(2,1)}, u32[]{:S(2)}, u32[]{:S(2)}) collective-permute-start(bf16[128,2,8,128]{3,2,1,0:T(8,128)(2,1)} %get-tuple-element.69), channel_id=1, source_target_pairs={{0,2},{2,0},{4,6},{6,4},{8,10},{10,8},{12,14},{14,12},{16,18},{18,... | collective-permute-start | bytes 1572872 | tf_op jit(solution)/shard_map/ppermute | solution.py:61
  45.0 2.4 %collective-permute-start.14 = (bf16[128,2,8,128]{3,2,1,0:T(8,128)(2,1)}, bf16[128,2,8,128]{3,2,1,0:T(8,128)(2,1)}, u32[]{:S(2)}, u32[]{:S(2)}) collective-permute-start(bf16[128,2,8,128]{3,2,1,0:T(8,128)(2,1)} %get-tuple-element.70), channel_id=1, source_target_pairs={{0,32},{2,4},{4,2},{6,8},{8,6},{10,12},{12,10},{14,46},{16,48},{18... | collective-permute-start | bytes 1572872 | tf_op jit(solution)/shard_map/ppermute | solution.py:61
  47.5 12.4 %collective-permute-done.10.refs_3_ = bf16[64,2,16,128]{3,2,1,0:T(8,128)(2,1)} collective-permute-done((bf16[64,2,16,128]{3,2,1,0:T(8,128)(2,1)S(1)}, bf16[64,2,16,128]{3,2,1,0:T(8,128)(2,1)}, u32[]{:S(2)}, u32[]{:S(2)}) %collective-permute-start.10) | collective-permute-done | bytes 524320 | tf_op jit(solution)/shard_map/ppermute | solution.py:69
  59.9 0.0 collective-permute-start.11
  59.9 0.0 collective-permute-done.9.refs_2_
  59.9 3.2 %collective-permute-start.12 = (bf16[128,2,8,128]{3,2,1,0:T(8,128)(2,1)}, bf16[128,2,8,128]{3,2,1,0:T(8,128)(2,1)}, u32[]{:S(2)}, u32[]{:S(2)}) collective-permute-start(bf16[128,2,8,128]{3,2,1,0:T(8,128)(2,1)} %get-tuple-element.66), channel_id=1, source_target_pairs={{0,32},{2,4},{4,2},{6,8},{8,6},{10,12},{12,10},{14,46},{16,48},{18... | collective-permute-start | bytes 1572872 | tf_op jit(solution)/shard_map/ppermute | solution.py:61
  63.1 2.4 %halo_to_heads.1 = (bf16[16,2,64,128]{3,2,1,0:T(8,128)(2,1)}, bf16[16,2,64,128]{3,2,1,0:T(8,128)(2,1)}) custom-call(s32[2]{0:T(128)} %pad_add_fusion.even, bf16[64,2,16,128]{3,2,1,0:T(8,128)(2,1)} %collective-permute-done.3.x.a, bf16[64,2,16,128]{3,2,1,0:T(8,128)(2,1)} %collective-permute-done.4.y.b), custom_call_target="tpu_custom_call" | custom-call | tf_op jit(solution)/shard_map/halo_to_heads/pallas_call | solution.py:115
  65.5 0.0 collective-permute-done.8.refs_1_
  65.5 2.8 %far_heads.1.far = bf16[16,2,256,128]{3,2,1,0:T(8,128)(2,1)} custom-call(bf16[64,2,16,128]{3,2,1,0:T(8,128)(2,1)} %copy-done, bf16[64,2,16,128]{3,2,1,0:T(8,128)(2,1)} %collective-permute-done.8.refs_1_, bf16[64,2,16,128]{3,2,1,0:T(8,128)(2,1)} %collective-permute-done.9.refs_2_, bf16[64,2,16,128]{3,2,1,0:T(8,128)(2,1)} %collective-permute-done.10.refs_3_), custom_call_target="tpu_custom_call" | custom-call | tf_op jit(solution)/shard_map/far_heads/pallas_call | solution.py:136
  68.3 0.0 collective-permute-done.13.sa
  68.3 0.0 collective-permute-done.14.sb
  68.3 11.9 %attend.3 = (bf16[8,384,128]{2,1,0:T(8,128)(2,1)}, bf16[8,384,128]{2,1,0:T(8,128)(2,1)}, bf16[8,2,384,128]{3,2,1,0:T(8,128)(2,1)}, bf16[8,2,64,128]{3,2,1,0:T(8,...) custom-call(bf16[16,384,128]{2,1,0:T(8,128)(2,1)} %get-tuple-element., ...), custom_call_target="tpu_custom_call" | custom-call | flops 2617245696 | bytes 12582912 | tf_op jit(solution)/shard_map/attend/pallas_call | solution.py:399
  80.2 0.1 collective-permute-start.16
  80.3 2.0 %collective-permute-start.18 = (bf16[8,2,128,128]{3,2,1,0:T(8,128)(2,1)}, bf16[8,2,128,128]{3,2,1,0:T(8,128)(2,1)}, u32[]{:S(2)}, u32[]{:S(2)}) collective-permute-start(bf16[8,2,128,128]{3,2,1,0:T(8,128)(2,1)} %get-tuple-element.81), channel_id=1, source_target_pairs={{0,32},{2,4},{4,2},{6,8},{8,6},{10,12},{12,10},{14,46},{16,48},{18... | collective-permute-start | bytes 1572872 | tf_op jit(solution)/shard_map/ppermute | solution.py:61
  82.3 0.0 collective-permute-done.11.sa
  82.3 0.0 collective-permute-done.12.sb
  82.4 11.9 %attend.2 = (bf16[8,384,128]{2,1,0:T(8,128)(2,1)}, bf16[8,384,128]{2,1,0:T(8,128)(2,1)}, bf16[8,2,384,128]{3,2,1,0:T(8,128)(2,1)}, bf16[8,2,64,128]{3,2,1,0:T(8,...) custom-call(bf16[16,384,128]{2,1,0:T(8,128)(2,1)} %get-tuple-element., ...), custom_call_target="tpu_custom_call" | custom-call | flops 2617245696 | bytes 12582912 | tf_op jit(solution)/shard_map/attend/pallas_call | solution.py:399
  94.2 0.1 collective-permute-start.15
  94.3 4.1 %collective-permute-start.17 = (bf16[8,2,128,128]{3,2,1,0:T(8,128)(2,1)}, bf16[8,2,128,128]{3,2,1,0:T(8,128)(2,1)}, u32[]{:S(2)}, u32[]{:S(2)}) collective-permute-start(bf16[8,2,128,128]{3,2,1,0:T(8,128)(2,1)} %get-tuple-element.80), channel_id=1, source_target_pairs={{0,32},{2,4},{4,2},{6,8},{8,6},{10,12},{12,10},{14,46},{16,48},{18... | collective-permute-start | bytes 1572872 | tf_op jit(solution)/shard_map/ppermute | solution.py:61
  98.4 0.0 collective-permute-done.16.refs_3_.refs_5_
  98.4 0.0 collective-permute-done.18.refs_5_.refs_7_
  98.5 8.7 %collective-permute-done.15.refs_2_.refs_4_ = bf16[8,2,128,128]{3,2,1,0:T(8,128)(2,1)} collective-permute-done((bf16[8,2,128,128]{3,2,1,0:T(8,128)(2,1)}, bf16[8,2,128,128]{3,2,1,0:T(8,128)(2,1)}, u32[]{:S(2)}, u32[]{:S(2)}) %collective-permute-start.15) | collective-permute-done | bytes 524320 | tf_op jit(solution)/shard_map/ppermute | solution.py:61
  107.1 2.2 %collective-permute-done.17.refs_4_.refs_6_ = bf16[8,2,128,128]{3,2,1,0:T(8,128)(2,1)} collective-permute-done((bf16[8,2,128,128]{3,2,1,0:T(8,128)(2,1)}, bf16[8,2,128,128]{3,2,1,0:T(8,128)(2,1)}, u32[]{:S(2)}, u32[]{:S(2)}) %collective-permute-start.17) | collective-permute-done | bytes 524320 | tf_op jit(solution)/shard_map/ppermute | solution.py:61
  109.4 3.2 %fold.1 = (bf16[64,2,16,128]{3,2,1,0:T(8,128)(2,1)}, bf16[64,2,16,128]{3,2,1,0:T(8,128)(2,1)}) custom-call(s32[2]{0:T(128)} %pad_add_fusion.even, bf16[8,2,64,128]{3,2,1,0:T(8,128)(2,1)} %get-tuple-element.84.refs_0_, bf16[8,2,64,128]{3,2,1,0:T(8,128)(2,1)} %get-tuple-element.85.refs_1_, bf16[8,2,64,128]{3,2,1,0:T(8,128)(2,1)} %get-tuple-element.86.refs_2_, ...), custom_call_target="tpu_custom_call" | custom-call | tf_op jit(solution)/shard_map/fold/pallas_call | solution.py:232
  112.6 1.4 %collective-permute-start.19 = (bf16[64,2,16,128]{3,2,1,0:T(8,128)(2,1)}, bf16[64,2,16,128]{3,2,1,0:T(8,128)(2,1)S(1)}, u32[]{:S(2)}, u32[]{:S(2)}) collective-permute-start(bf16[64,2,16,128]{3,2,1,0:T(8,128)(2,1)} %get-tuple-element.88), channel_id=1, source_target_pairs={{0,16},{2,18},{4,20},{6,22},{8,24},{10,26},{12,28},{14,30},{16,0},... | collective-permute-start | bytes 1572872 | tf_op jit(solution)/shard_map/ppermute | solution.py:61
  114.0 7.7 %collective-permute-start.20 = (bf16[64,2,16,128]{3,2,1,0:T(8,128)(2,1)}, bf16[64,2,16,128]{3,2,1,0:T(8,128)(2,1)}, u32[]{:S(2)}, u32[]{:S(2)}) collective-permute-start(bf16[64,2,16,128]{3,2,1,0:T(8,128)(2,1)} %get-tuple-element.89), channel_id=1, source_target_pairs={{0,0},{2,2},{4,4},{6,6},{8,8},{10,10},{12,12},{14,14},{16,32},{18,... | collective-permute-start | bytes 1572872 | tf_op jit(solution)/shard_map/ppermute | solution.py:61
  121.8 4.0 %to_tokens.1 = (bf16[1,384,16,128]{3,2,1,0:T(8,128)(2,1)}, bf16[1,384,16,128]{3,2,1,0:T(8,128)(2,1)}) custom-call(bf16[8,384,128]{2,1,0:T(8,128)(2,1)} %get-tuple-element.68.refs_0_, bf16[8,384,128]{2,1,0:T(8,128)(2,1)} %get-tuple-element.71.refs_1_, bf16[8,384,128]{2,1,0:T(8,128)(2,1)} %get-tuple-element.72.refs_2_, ...), custom_call_target="tpu_custom_call" | custom-call | tf_op jit(solution)/shard_map/to_tokens/pallas_call | solution.py:197
  125.8 5.7 %premerge.1 = (bf16[1,384,16,128]{3,2,1,0:T(8,128)(2,1)}, bf16[1,384,16,128]{3,2,1,0:T(8,128)(2,1)}) custom-call(s32[2]{0:T(128)} %pad_add_fusion.even, bf16[8,2,384,128]{3,2,1,0:T(8,128)(2,1)} %get-tuple-element.76.refs_0_, bf16[8,2,384,128]{3,2,1,0:T(8,128)(2,1)} %get-tuple-element.77.refs_1_, ...), custom_call_target="tpu_custom_call" | custom-call | tf_op jit(solution)/shard_map/premerge/pallas_call | solution.py:266
  131.4 5.8 %collective-permute-done.19.from_a = bf16[64,2,16,128]{3,2,1,0:T(8,128)(2,1)S(1)} collective-permute-done((bf16[64,2,16,128]{3,2,1,0:T(8,128)(2,1)}, bf16[64,2,16,128]{3,2,1,0:T(8,128)(2,1)S(1)}, u32[]{:S(2)}, u32[]{:S(2)}) %collective-permute-start.19) | collective-permute-done | bytes 524320 | tf_op jit(solution)/shard_map/ppermute | solution.py:61
  137.2 0.0 collective-permute-done.20.from_b
  137.2 0.8 copy-done.2
  138.1 3.2 %finish.1 = (bf16[1,384,16,128]{3,2,1,0:T(8,128)(2,1)}, bf16[1,384,16,128]{3,2,1,0:T(8,128)(2,1)}) custom-call(s32[2]{0:T(128)} %pad_add_fusion.even, bf16[1,384,16,128]{3,2,1,0:T(8,128)(2,1)} %get-tuple-element.82.dk, bf16[1,384,16,128]{3,2,1,0:T(8,128)(2,1)} %get-tuple-element.83.dv, ...), custom_call_target="tpu_custom_call", output_to_operand_aliasing={{0}: (1, {}), {1}: (2, {})} | custom-call | tf_op jit(solution)/shard_map/finish/pallas_call | solution.py:289
  (18 shorter events, 0.1 us)
Async XLA Ops:
  1.4 7.3 %collective-permute-start.2 = (bf16[4,2,16,128]{3,2,1,0:T(8,128)(2,1)S(1)}, bf16[4,2,16,128]{3,2,1,0:T(8,128)(2,1)S(1)}, u32[]{:S(2)}, u32[]{:S(2)}) collective-permute-start(bf16[4,2,16,128]{3,2,1,0:T(8,128)(2,1)S(1)} %pad_maximum_fusion.4), channel_id=1, source_target_pairs={{0,24},{2,26},{4,28},{6,30},{8,16},{10,18},{12,20},{14,22},{16,8},... | collective-permute-start | bytes 98312 | tf_op jit(solution)/shard_map/ppermute | solution.py:69
  3.6 5.4 %collective-permute-start.1 = (bf16[4,2,16,128]{3,2,1,0:T(8,128)(2,1)S(1)}, bf16[4,2,16,128]{3,2,1,0:T(8,128)(2,1)S(1)}, u32[]{:S(2)}, u32[]{:S(2)}) collective-permute-start(bf16[4,2,16,128]{3,2,1,0:T(8,128)(2,1)S(1)} %pad_maximum_fusion.4), channel_id=1, source_target_pairs={{0,16},{2,18},{4,20},{6,22},{8,24},{10,26},{12,28},{14,30},{16,0},... | collective-permute-start | bytes 98312 | tf_op jit(solution)/shard_map/ppermute | solution.py:69
  4.3 4.7 %collective-permute-start = (bf16[4,2,16,128]{3,2,1,0:T(8,128)(2,1)S(1)}, bf16[4,2,16,128]{3,2,1,0:T(8,128)(2,1)S(1)}, u32[]{:S(2)}, u32[]{:S(2)}) collective-permute-start(bf16[4,2,16,128]{3,2,1,0:T(8,128)(2,1)S(1)} %pad_maximum_fusion.4), channel_id=1, source_target_pairs={{0,8},{2,10},{4,12},{6,14},{8,0},{10,2},{12,4},{14,6},{16,24},{18,... | collective-permute-start | bytes 98312 | tf_op jit(solution)/shard_map/ppermute | solution.py:69
  7.0 2.1 %copy-start.3 = (bf16[1,4,16,128]{3,2,1,0:T(8,128)(2,1)S(1)}, bf16[1,4,16,128]{3,2,1,0:T(8,128)(2,1)}, u32[]{:S(2)}) copy-start(bf16[1,4,16,128]{3,2,1,0:T(8,128)(2,1)} %param.10) | copy-start | bytes 49156
  7.0 2.0 %copy-start.4 = (bf16[1,4,16,128]{3,2,1,0:T(8,128)(2,1)S(1)}, bf16[1,4,16,128]{3,2,1,0:T(8,128)(2,1)}, u32[]{:S(2)}) copy-start(bf16[1,4,16,128]{3,2,1,0:T(8,128)(2,1)} %param.9) | copy-start | bytes 49156
  9.0 11.9 %collective-permute-start.7 = (bf16[16,2,16,128]{3,2,1,0:T(8,128)(2,1)S(1)}, bf16[16,2,16,128]{3,2,1,0:T(8,128)(2,1)S(1)}, u32[]{:S(2)}, u32[]{:S(2)}) collective-permute-start(bf16[16,2,16,128]{3,2,1,0:T(8,128)(2,1)S(1)} %pad_maximum_fusion.3), channel_id=1, source_target_pairs={{0,96},{2,98},{4,100},{6,102},{8,104},{10,106},{12,108},{14,110},{... | collective-permute-start | bytes 393224 | tf_op jit(solution)/shard_map/ppermute | solution.py:69
  13.4 9.7 %collective-permute-start.6 = (bf16[16,2,16,128]{3,2,1,0:T(8,128)(2,1)S(1)}, bf16[16,2,16,128]{3,2,1,0:T(8,128)(2,1)S(1)}, u32[]{:S(2)}, u32[]{:S(2)}) collective-permute-start(bf16[16,2,16,128]{3,2,1,0:T(8,128)(2,1)S(1)} %pad_maximum_fusion.3), channel_id=1, source_target_pairs={{0,64},{2,66},{4,68},{6,70},{8,72},{10,74},{12,76},{14,78},{16,80}... | collective-permute-start | bytes 393224 | tf_op jit(solution)/shard_map/ppermute | solution.py:69
  13.4 9.7 %collective-permute-start.5 = (bf16[16,2,16,128]{3,2,1,0:T(8,128)(2,1)S(1)}, bf16[16,2,16,128]{3,2,1,0:T(8,128)(2,1)S(1)}, u32[]{:S(2)}, u32[]{:S(2)}) collective-permute-start(bf16[16,2,16,128]{3,2,1,0:T(8,128)(2,1)S(1)} %pad_maximum_fusion.3), channel_id=1, source_target_pairs={{0,32},{2,34},{4,36},{6,38},{8,40},{10,42},{12,44},{14,46},{16,48}... | collective-permute-start | bytes 393224 | tf_op jit(solution)/shard_map/ppermute | solution.py:69
  14.1 25.3 %collective-permute-start.3 = (bf16[64,2,16,128]{3,2,1,0:T(8,128)(2,1)}, bf16[64,2,16,128]{3,2,1,0:T(8,128)(2,1)}, u32[]{:S(2)}, u32[]{:S(2)}) collective-permute-start(bf16[64,2,16,128]{3,2,1,0:T(8,128)(2,1)} %pad_maximum_fusion), channel_id=1, source_target_pairs={{0,16},{2,18},{4,20},{6,22},{8,24},{10,26},{12,28},{14,30},{16,0},... | collective-permute-start | bytes 1572872 | tf_op jit(solution)/shard_map/ppermute | solution.py:61
  15.5 23.9 %collective-permute-start.4 = (bf16[64,2,16,128]{3,2,1,0:T(8,128)(2,1)}, bf16[64,2,16,128]{3,2,1,0:T(8,128)(2,1)}, u32[]{:S(2)}, u32[]{:S(2)}) collective-permute-start(bf16[64,2,16,128]{3,2,1,0:T(8,128)(2,1)} %pad_maximum_fusion.1), channel_id=1, source_target_pairs={{0,0},{2,2},{4,4},{6,6},{8,8},{10,10},{12,12},{14,14},{16,32},{18,... | collective-permute-start | bytes 1572872 | tf_op jit(solution)/shard_map/ppermute | solution.py:61
  23.2 10.0 %copy-start = (bf16[64,2,16,128]{3,2,1,0:T(8,128)(2,1)}, bf16[64,2,16,128]{3,2,1,0:T(8,128)(2,1)S(1)}, u32[]{:S(2)}) copy-start(bf16[64,2,16,128]{3,2,1,0:T(8,128)(2,1)S(1)} %pad_maximum_fusion.2.refs_0_) | copy-start | bytes 1572868
  23.3 36.6 %collective-permute-start.10 = (bf16[64,2,16,128]{3,2,1,0:T(8,128)(2,1)S(1)}, bf16[64,2,16,128]{3,2,1,0:T(8,128)(2,1)}, u32[]{:S(2)}, u32[]{:S(2)}) collective-permute-start(bf16[64,2,16,128]{3,2,1,0:T(8,128)(2,1)S(1)} %pad_maximum_fusion.2.refs_0_), channel_id=1, source_target_pairs={{0,6},{2,4},{4,2},{6,0},{8,14},{10,12},{12,10},{14,8},{16,22},{18,... | collective-permute-start | bytes 1572872 | tf_op jit(solution)/shard_map/ppermute | solution.py:69
  26.4 33.5 %collective-permute-start.9 = (bf16[64,2,16,128]{3,2,1,0:T(8,128)(2,1)S(1)}, bf16[64,2,16,128]{3,2,1,0:T(8,128)(2,1)}, u32[]{:S(2)}, u32[]{:S(2)}) collective-permute-start(bf16[64,2,16,128]{3,2,1,0:T(8,128)(2,1)S(1)} %pad_maximum_fusion.2.refs_0_), channel_id=1, source_target_pairs={{0,4},{2,6},{4,0},{6,2},{8,12},{10,14},{12,8},{14,10},{16,20},{18,... | collective-permute-start | bytes 1572872 | tf_op jit(solution)/shard_map/ppermute | solution.py:69
  28.1 37.4 %collective-permute-start.8 = (bf16[64,2,16,128]{3,2,1,0:T(8,128)(2,1)S(1)}, bf16[64,2,16,128]{3,2,1,0:T(8,128)(2,1)}, u32[]{:S(2)}, u32[]{:S(2)}) collective-permute-start(bf16[64,2,16,128]{3,2,1,0:T(8,128)(2,1)S(1)} %pad_maximum_fusion.2.refs_0_), channel_id=1, source_target_pairs={{0,2},{2,0},{4,6},{6,4},{8,10},{10,8},{12,14},{14,12},{16,18},{18,... | collective-permute-start | bytes 1572872 | tf_op jit(solution)/shard_map/ppermute | solution.py:69
  43.5 24.9 %collective-permute-start.13 = (bf16[128,2,8,128]{3,2,1,0:T(8,128)(2,1)}, bf16[128,2,8,128]{3,2,1,0:T(8,128)(2,1)}, u32[]{:S(2)}, u32[]{:S(2)}) collective-permute-start(bf16[128,2,8,128]{3,2,1,0:T(8,128)(2,1)} %get-tuple-element.69), channel_id=1, source_target_pairs={{0,2},{2,0},{4,6},{6,4},{8,10},{10,8},{12,14},{14,12},{16,18},{18,... | collective-permute-start | bytes 1572872 | tf_op jit(solution)/shard_map/ppermute | solution.py:61
  45.0 23.3 %collective-permute-start.14 = (bf16[128,2,8,128]{3,2,1,0:T(8,128)(2,1)}, bf16[128,2,8,128]{3,2,1,0:T(8,128)(2,1)}, u32[]{:S(2)}, u32[]{:S(2)}) collective-permute-start(bf16[128,2,8,128]{3,2,1,0:T(8,128)(2,1)} %get-tuple-element.70), channel_id=1, source_target_pairs={{0,32},{2,4},{4,2},{6,8},{8,6},{10,12},{12,10},{14,46},{16,48},{18... | collective-permute-start | bytes 1572872 | tf_op jit(solution)/shard_map/ppermute | solution.py:61
  59.9 22.5 %collective-permute-start.11 = (bf16[128,2,8,128]{3,2,1,0:T(8,128)(2,1)}, bf16[128,2,8,128]{3,2,1,0:T(8,128)(2,1)}, u32[]{:S(2)}, u32[]{:S(2)}) collective-permute-start(bf16[128,2,8,128]{3,2,1,0:T(8,128)(2,1)} %get-tuple-element.65), channel_id=1, source_target_pairs={{0,2},{2,0},{4,6},{6,4},{8,10},{10,8},{12,14},{14,12},{16,18},{18,... | collective-permute-start | bytes 1572872 | tf_op jit(solution)/shard_map/ppermute | solution.py:61
  59.9 22.5 %collective-permute-start.12 = (bf16[128,2,8,128]{3,2,1,0:T(8,128)(2,1)}, bf16[128,2,8,128]{3,2,1,0:T(8,128)(2,1)}, u32[]{:S(2)}, u32[]{:S(2)}) collective-permute-start(bf16[128,2,8,128]{3,2,1,0:T(8,128)(2,1)} %get-tuple-element.66), channel_id=1, source_target_pairs={{0,32},{2,4},{4,2},{6,8},{8,6},{10,12},{12,10},{14,46},{16,48},{18... | collective-permute-start | bytes 1572872 | tf_op jit(solution)/shard_map/ppermute | solution.py:61
  80.2 18.2 %collective-permute-start.16 = (bf16[8,2,128,128]{3,2,1,0:T(8,128)(2,1)}, bf16[8,2,128,128]{3,2,1,0:T(8,128)(2,1)S(1)}, u32[]{:S(2)}, u32[]{:S(2)}) collective-permute-start(bf16[8,2,128,128]{3,2,1,0:T(8,128)(2,1)} %get-tuple-element.79), channel_id=1, source_target_pairs={{0,2},{2,0},{4,6},{6,4},{8,10},{10,8},{12,14},{14,12},{16,18},{18,... | collective-permute-start | bytes 1572872 | tf_op jit(solution)/shard_map/ppermute | solution.py:61
  80.3 18.1 %collective-permute-start.18 = (bf16[8,2,128,128]{3,2,1,0:T(8,128)(2,1)}, bf16[8,2,128,128]{3,2,1,0:T(8,128)(2,1)}, u32[]{:S(2)}, u32[]{:S(2)}) collective-permute-start(bf16[8,2,128,128]{3,2,1,0:T(8,128)(2,1)} %get-tuple-element.81), channel_id=1, source_target_pairs={{0,32},{2,4},{4,2},{6,8},{8,6},{10,12},{12,10},{14,46},{16,48},{18... | collective-permute-start | bytes 1572872 | tf_op jit(solution)/shard_map/ppermute | solution.py:61
  94.2 12.9 %collective-permute-start.15 = (bf16[8,2,128,128]{3,2,1,0:T(8,128)(2,1)}, bf16[8,2,128,128]{3,2,1,0:T(8,128)(2,1)}, u32[]{:S(2)}, u32[]{:S(2)}) collective-permute-start(bf16[8,2,128,128]{3,2,1,0:T(8,128)(2,1)} %get-tuple-element.78), channel_id=1, source_target_pairs={{0,2},{2,0},{4,6},{6,4},{8,10},{10,8},{12,14},{14,12},{16,18},{18,... | collective-permute-start | bytes 1572872 | tf_op jit(solution)/shard_map/ppermute | solution.py:61
  94.3 15.0 %collective-permute-start.17 = (bf16[8,2,128,128]{3,2,1,0:T(8,128)(2,1)}, bf16[8,2,128,128]{3,2,1,0:T(8,128)(2,1)}, u32[]{:S(2)}, u32[]{:S(2)}) collective-permute-start(bf16[8,2,128,128]{3,2,1,0:T(8,128)(2,1)} %get-tuple-element.80), channel_id=1, source_target_pairs={{0,32},{2,4},{4,2},{6,8},{8,6},{10,12},{12,10},{14,46},{16,48},{18... | collective-permute-start | bytes 1572872 | tf_op jit(solution)/shard_map/ppermute | solution.py:61
  98.4 10.9 %copy-start.1 = (bf16[8,2,128,128]{3,2,1,0:T(8,128)(2,1)}, bf16[8,2,128,128]{3,2,1,0:T(8,128)(2,1)S(1)}, u32[]{:S(2)}) copy-start(bf16[8,2,128,128]{3,2,1,0:T(8,128)(2,1)S(1)} %collective-permute-done.16.refs_3_.refs_5_) | copy-start | bytes 1572868
  112.6 24.6 %collective-permute-start.19 = (bf16[64,2,16,128]{3,2,1,0:T(8,128)(2,1)}, bf16[64,2,16,128]{3,2,1,0:T(8,128)(2,1)S(1)}, u32[]{:S(2)}, u32[]{:S(2)}) collective-permute-start(bf16[64,2,16,128]{3,2,1,0:T(8,128)(2,1)} %get-tuple-element.88), channel_id=1, source_target_pairs={{0,16},{2,18},{4,20},{6,22},{8,24},{10,26},{12,28},{14,30},{16,0},... | collective-permute-start | bytes 1572872 | tf_op jit(solution)/shard_map/ppermute | solution.py:61
  114.0 23.2 %collective-permute-start.20 = (bf16[64,2,16,128]{3,2,1,0:T(8,128)(2,1)}, bf16[64,2,16,128]{3,2,1,0:T(8,128)(2,1)}, u32[]{:S(2)}, u32[]{:S(2)}) collective-permute-start(bf16[64,2,16,128]{3,2,1,0:T(8,128)(2,1)} %get-tuple-element.89), channel_id=1, source_target_pairs={{0,0},{2,2},{4,4},{6,6},{8,8},{10,10},{12,12},{14,14},{16,32},{18,... | collective-permute-start | bytes 1572872 | tf_op jit(solution)/shard_map/ppermute | solution.py:61
  137.2 0.8 copy-start.2
